TPU v7x, 32 devices: a whole 2x2x4 slice. The times are simulated.
32 devices in a mesh: parts: 2 (over y), seq: 4 (over z), res: 4 (over x, core).
Axes of the slice: x: 2, y: 2, z: 4, core: 2. Of those that a mesh axis runs over, the one named last changes fastest.
Arguments:
- relatives_stack: bfloat16 [128, 64, 256], P(('parts', 'seq'), 'res'), parts along dimension 0, may hold values from -6 to 6
- edge_embedding: bfloat16 [128, 64, 128], P(('parts', 'res'), 'seq'), parts along dimension 0, may hold values from -6 to 6
- homolog_present: int32 [128, 64], P(('parts', 'seq'), 'res'), parts along dimension 0, may hold values 0 or 1
- amino_present: int32 [128], P(('parts', 'res')), parts along dimension 0, may hold values 0 or 1
- relatives_stretch: float32 [256], replicated, may hold values from 0.1 to 1.9
- joint_qkvg_weights: bfloat16 [256, 1024], replicated, may hold values from -0.375 to 0.375
- edge_to_logit_matrix: float32 [128, 8], replicated, may hold values from -100 to 100
- closing_blend_weights: bfloat16 [256, 256], replicated, may hold values from -2 to 2
- operand_weights: bfloat16 [256, 64], replicated, may hold values from -0.375 to 0.375
- product_to_edge_matrix: bfloat16 [1024, 128], replicated, may hold values from -6 to 6
Outputs:
- attended_stack: bfloat16 [128, 64, 256], P(('parts', 'seq'), 'res'), parts along dimension 0
- pair_output: bfloat16 [128, 64, 128], P(('parts', 'res'), 'seq'), parts along dimension 0
There are 2 independent parts, one for each index of `parts`. A program takes and returns all parts, laid end to end along the dimension named above; an argument that names none is the same for every part. Nothing has to cross between parts.
All inputs are finite; a program needn't handle non-finite values. No bound on the sum of `homolog_present` or of `amino_present` on one device may be relied on, other than what follows from the above.
Results may differ from a plain program's by a relative error of at most 0.019.
The roundings to bfloat16 on the way count: a program that leaves them out, or rounds other values in their place, can miss the bound.
Values may be sent and summed in bfloat16 or wider, within the bound.
A program may use at most 64 MiB of HBM per device.

v0:
```python
import math

import jax
import jax.numpy as jnp
from jax import lax
from jax.sharding import PartitionSpec as P


def standardize_features(values):
    center = jnp.mean(values, axis=-1, keepdims=True)
    shifted = values - center
    spread = jnp.mean(shifted * shifted, axis=-1, keepdims=True)
    return shifted * lax.rsqrt(spread + 1e-05)


def attend(queries, key_rows, value_rows, usable, bias_block):
    scores = jnp.einsum("nihd,njhd->nhij", queries, key_rows, preferred_element_type=jnp.float32)
    scores = scores + jnp.transpose(bias_block.astype(jnp.float32), (2, 0, 1))[None]
    scores = jnp.where(usable[:, None, None, :] > 0, scores, -1000000000.0)
    ceiling = jnp.max(scores, axis=-1, keepdims=True)
    raised = jnp.exp(scores - ceiling)
    weights = (raised / jnp.sum(raised, axis=-1, keepdims=True)).astype(jnp.bfloat16)
    return jnp.einsum(
        "nhij,njhd->nihd", weights, value_rows, preferred_element_type=jnp.float32
    ).astype(jnp.bfloat16)


def shards(
    relatives_stack,
    edge_embedding,
    homolog_present,
    amino_present,
    relatives_stretch,
    joint_qkvg_weights,
    edge_to_logit_matrix,
    closing_blend_weights,
    operand_weights,
    product_to_edge_matrix,
):
    homolog_lines, amino_acid_lines, feature_product_size = relatives_stack.shape
    head_count = edge_to_logit_matrix.shape[1]
    head_width = closing_blend_weights.shape[0] // head_count
    columns = edge_embedding.shape[1]
    valid_entries = (homolog_present * amino_present[None, :]).astype(jnp.bfloat16)
    whitened_stack = (
        standardize_features(relatives_stack.astype(jnp.float32)) * relatives_stretch
    ).astype(jnp.bfloat16)
    blended_groups = jnp.dot(
        whitened_stack.reshape(-1, feature_product_size),
        joint_qkvg_weights,
        preferred_element_type=jnp.float32,
    )
    blended_groups = blended_groups.reshape(
        homolog_lines, amino_acid_lines, 4, head_count, head_width
    )
    scale = 1.0 / math.sqrt(head_width)
    queries = (blended_groups[:, :, 0] * scale).astype(jnp.bfloat16)
    key_rows = blended_groups[:, :, 1].astype(jnp.bfloat16)
    value_rows = blended_groups[:, :, 2].astype(jnp.bfloat16)
    gating = jax.nn.sigmoid(blended_groups[:, :, 3])
    pair_normed = standardize_features(edge_embedding.astype(jnp.float32)).reshape(
        -1, edge_embedding.shape[2]
    )
    local_bias = jnp.dot(pair_normed, edge_to_logit_matrix, precision=lax.Precision.HIGHEST)
    local_bias = local_bias.reshape(amino_acid_lines, columns, head_count).astype(jnp.bfloat16)
    full_bias = lax.all_gather(local_bias, "seq", axis=1, tiled=True)
    all_keys, all_values, all_valid = (
        lax.all_gather(key_rows, "res", axis=1, tiled=True),
        lax.all_gather(value_rows, "res", axis=1, tiled=True),
        lax.all_gather(valid_entries, "res", axis=1, tiled=True),
    )
    attended = attend(queries, all_keys, all_values, all_valid, full_bias)
    gated_values = (
        (gating * attended.astype(jnp.float32))
        .astype(jnp.bfloat16)
        .reshape(-1, head_count * head_width)
    )
    relatives_folded = relatives_stack.astype(jnp.float32).reshape(-1, feature_product_size)
    attended_stack = (
        relatives_folded
        + jnp.dot(gated_values, closing_blend_weights, preferred_element_type=jnp.float32)
    ).astype(jnp.bfloat16)
    attended_stack = attended_stack.reshape(homolog_lines, amino_acid_lines, feature_product_size)
    tensor_averaged = standardize_features(attended_stack.astype(jnp.float32)).astype(jnp.bfloat16)
    outer_width = operand_weights.shape[1] // 2
    operand_couples = jnp.dot(
        tensor_averaged.reshape(-1, feature_product_size),
        operand_weights,
        preferred_element_type=jnp.float32,
    )
    operand_couples = operand_couples.reshape(
        homolog_lines, amino_acid_lines, 2 * outer_width
    ) * valid_entries[:, :, None].astype(jnp.float32)
    operand_couples = operand_couples.astype(jnp.bfloat16)
    left = operand_couples[:, :, :outer_width]
    right = operand_couples[:, :, outer_width:]
    all_right, right_valid = (
        lax.all_gather(right, "res", axis=1, tiled=True),
        lax.all_gather(valid_entries, "res", axis=1, tiled=True),
    )
    proj_wide = product_to_edge_matrix.astype(jnp.float32)
    own_start = lax.axis_index("seq") * columns
    block = jnp.einsum("sip,sjq->jipq", left, all_right, preferred_element_type=jnp.float32)
    block = block.reshape(
        columns * lax.axis_size("seq") * amino_acid_lines, outer_width * outer_width
    )
    owned = lax.psum_scatter(
        jnp.dot(block, proj_wide, precision=lax.Precision.HIGHEST).reshape(
            columns * lax.axis_size("seq"), amino_acid_lines, -1
        ),
        "seq",
        scatter_dimension=0,
        tiled=True,
    )
    update = jnp.transpose(owned, (1, 0, 2))
    own_counts = jnp.dot(valid_entries.T, right_valid, preferred_element_type=jnp.float32)
    count_sum = lax.psum(own_counts, "seq")
    counts = lax.dynamic_slice_in_dim(count_sum, own_start, columns, 1)
    pair_output = (
        edge_embedding.astype(jnp.float32) + update / jnp.maximum(counts, 1.0)[:, :, None]
    ).astype(jnp.bfloat16)
    return (attended_stack, pair_output)


def solution(mesh):
    in_specs = (
        P(("parts", "seq"), "res", None),
        P(("parts", "res"), "seq", None),
        P(("parts", "seq"), "res"),
        P(("parts", "res")),
        P(),
        P(),
        P(),
        P(),
        P(),
        P(),
    )
    out_specs = (P(("parts", "seq"), "res", None), P(("parts", "res"), "seq", None))
    return jax.shard_map(shards, mesh=mesh, in_specs=in_specs, out_specs=out_specs, check_vma=False)
```

profile of v0, /device:TPU:0, one launch (start us, length us, event | category | flops | bytes accessed | tf_op | source)
XLA Modules:
  0.0 135.2 jit_solution(5903399821607846803)
XLA Ops:
  7.2 0.8 copy.53
  8.0 0.7 multiply_convert_fusion.1
  8.8 0.7 copy.60
  9.4 6.2 %all_gather.17 = bf16[16,64]{0,1:T(8,128)(2,1)S(1)} all-gather(bf16[16,16]{0,1:T(8,128)(2,1)S(1)} %multiply_convert_fusion.1), channel_id=1, replica_groups=mesh['parts'=2,'seq'=4,'res'=4] {'res'}, dimensions={1}, use_global_device_ids=true | all-gather | bytes 2560 | tf_op jit(solution)/shard_map/all_gather | solution.py:70
  15.6 1.0 convert_reduce_fusion.2
  16.6 1.1 multiply_reduce_fusion
  17.7 0.9 convert_reduce_fusion.1
  18.7 1.0 fusion.47
  19.9 1.9 %convolution_convert_fusion = bf16[16,16,8]{1,2,0:T(8,128)(2,1)S(1)} fusion(bf16[16,16,128]{2,1,0:T(8,128)(2,1)} %param.11, f32[16,16]{1,0:T(8,128)S(1)} %add_rsqrt_fusion, f32[16,16]{1,0:T(8,128)S(1)} %broadcast_multiply_fusion, f32[128,8]{0,1:T(8,128)} %param.16), kind=kOutput, calls=%fused_computation.19 | convolution fusion | flops 3246080 | bytes 75776 | tf_op jit(solution)/shard_map/dot_general | solution.py:64
  21.9 14.0 %all_gather.19 = bf16[16,64,8]{0,2,1:T(8,128)(2,1)S(1)} all-gather(bf16[16,16,8]{0,2,1:T(8,128)(2,1)S(1)} %copy.56), channel_id=1, replica_groups=mesh['parts'=2,'seq'=4,'res'=4] {'seq'}, dimensions={1}, use_global_device_ids=true | all-gather | bytes 20480 | tf_op jit(solution)/shard_map/all_gather | solution.py:66
  36.1 1.3 copy.52
  37.4 1.7 %fusion.66 = (bf16[16,16,4,8,32]{4,1,3,2,0:T(8,128)(2,1)S(1)}, f32[16,16,4,8,32]{4,1,3,2,0:T(8,128)S(1)}) fusion(bf16[4,8,32,256,1]{3,2,1,0,4:T(8,128)(2,1)S(1)} %bitcast.84, bf16[16,16,256]{2,1,0:T(8,128)(2,1)} %param.10, f32[256]{0:T(256)} %param.14, f32[16,16]{1,0:T(8,128)S(1)} %add_rsqrt_fusion.1, f32[16,16]{1,0:T(8,128)S(1)} %broadcast_multiply_fusion.1), kind=kOutput, calls=%fused_computation.75 | convolution fusion | flops 134807552 | bytes 2231296 | tf_op jit(solution)/shard_map/dot_general | solution.py:48
  39.1 0.2 fusion.64
  39.3 15.7 %all-gather.1 = bf16[16,64,1,8,32]{4,1,3,2,0:T(8,128)(2,1)S(1)} all-gather(bf16[16,16,1,8,32]{4,1,3,2,0:T(8,128)(2,1)S(1)} %get-tuple-element.6), channel_id=3, replica_groups=mesh['parts'=2,'seq'=4,'res'=4] {'res'}, dimensions={1}, use_global_device_ids=true | all-gather | bytes 655360 | tf_op jit(solution)/shard_map/all_gather | solution.py:68
  55.0 1.2 fusion.10
  56.2 1.3 fusion.67
  57.5 15.8 %all-gather = bf16[16,64,1,8,32]{4,1,3,2,0:T(8,128)(2,1)S(1)} all-gather(bf16[16,16,1,8,32]{4,1,3,2,0:T(8,128)(2,1)S(1)} %get-tuple-element.7), channel_id=2, replica_groups=mesh['parts'=2,'seq'=4,'res'=4] {'res'}, dimensions={1}, use_global_device_ids=true | all-gather | bytes 655360 | tf_op jit(solution)/shard_map/all_gather | solution.py:69
  73.3 5.8 %fusion.25 = bf16[16,16,8,32]{3,1,2,0:T(8,128)(2,1)} fusion(bf16[16,64,1,8,32]{4,1,3,2,0:T(8,128)(2,1)S(1)} %all-gather, f32[16,16,4,8,32]{4,1,3,2,0:T(8,128)} %copy-done.1, f32[16,8,16]{2,1,0:T(8,128)} %fusion.67, f32[16,8,16,64]{3,2,1,0:T(8,128)S(1)} %fusion.10), kind=kOutput, calls=%fused_computation.14 | convolution fusion | flops 9242687 | bytes 4595712 | tf_op jit(solution)/shard_map/nhij,njhd->nihd/dot_general | solution.py:23
  79.1 1.2 copy.59
  80.3 0.4 reshape.99
  80.7 1.2 convert_reduce_fusion
  81.9 0.2 fusion.41
  82.1 0.1 fusion.42
  82.2 0.9 fusion.29
  83.2 6.1 %all_gather.20 = bf16[16,64,32]{2,1,0:T(8,128)(2,1)S(1)} all-gather(bf16[16,16,32]{2,1,0:T(8,128)(2,1)S(1)} %get-tuple-element.9), channel_id=1, replica_groups=mesh['parts'=2,'seq'=4,'res'=4] {'res'}, dimensions={1}, use_global_device_ids=true | all-gather | bytes 81920 | tf_op jit(solution)/shard_map/all_gather | solution.py:98
  89.3 0.2 copy.68
  89.5 1.3 convolution_bitcast_fusion
  90.8 6.5 %copy.63 = f32[64,16,32,32]{0,3,2,1:T(8,128)S(1)} copy(f32[64,16,32,32]{0,2,1,3:T(8,128)S(1)} %convolution_bitcast_fusion) | data formatting | bytes 8388608 | tf_op jit(solution)/shard_map/sip,sjq->jipq/transpose | solution.py:103
  97.3 7.5 %fusion.43 = f32[64,16,128]{2,0,1:T(8,128)} fusion(f32[64,16,1024]{0,2,1:T(8,128)S(1)} %bitcast.83, bf16[1024,128]{1,0:T(8,128)(2,1)S(1)} %copy-done), kind=kOutput, calls=%fused_computation.37 | convolution fusion | flops 1610612736 | bytes 4980736 | tf_op jit(solution)/shard_map/dot_general | solution.py:108
  105.0 12.1 %psum.7 = f32[16,64]{1,0:T(8,128)S(1)} all-reduce(f32[16,64]{1,0:T(8,128)S(1)} %fusion.68), channel_id=1, replica_groups=mesh['parts'=2,'seq'=4,'res'=4] {'seq'}, use_global_device_ids=true, to_apply=%region_9.10 | all-reduce | flops 1024 | bytes 8192 | tf_op jit(solution)/shard_map/psum | solution.py:117
  117.1 9.6 %reduce-scatter.2.cloned.1.call-done = f32[16,16,128]{2,0,1:T(8,128)} async-done(((f32[64,16,128]{2,0,1:T(8,128)}), f32[16,16,128]{2,0,1:T(8,128)}) %reduce-scatter.2.cloned.1.call-update) | async-done | bytes 131088 | tf_op jit(solution)/shard_map/reduce_scatter | solution.py:107
  126.7 1.6 %fusion.49 = bf16[16,16,128]{2,1,0:T(8,128)(2,1)} fusion(bf16[16,16,128]{2,1,0:T(8,128)(2,1)S(1)} %copy-done.4, f32[16,16,128]{2,0,1:T(8,128)} %reduce-scatter.2.cloned.1.call-done, f32[16,16]{1,0:T(8,128)S(1)} %dynamic-slice_maximum_fusion), kind=kLoop, calls=%fused_computation.49 | loop fusion | flops 131072 | bytes 263168 | tf_op jit(solution)/shard_map/convert_element_type | solution.py:121
  (30 shorter events, 0.8 us)
Async XLA Ops:
  7.2 90.1 %copy-start = (bf16[1024,128]{1,0:T(8,128)(2,1)S(1)}, bf16[1024,128]{1,0:T(8,128)(2,1)}, u32[]{:S(2)}) copy-start(bf16[1024,128]{1,0:T(8,128)(2,1)} %param.19) | copy-start | bytes 786436
  7.2 119.5 %reduce-scatter.2.cloned.1.call-start = ((), (), s32[]{:S(2)}) async-start(), calls=%async_computation.1 | async-start | bytes 655360 | tf_op jit(solution)/shard_map/reduce_scatter | solution.py:107
  8.8 11.1 %copy-start.5 = (bf16[16,16]{0,1:T(8,128)(2,1)}, bf16[16,16]{0,1:T(8,128)(2,1)S(1)}, u32[]{:S(2)}) copy-start(bf16[16,16]{0,1:T(8,128)(2,1)S(1)} %multiply_convert_fusion.1) | copy-start | bytes 1540
  39.1 17.1 %copy-start.1 = (f32[16,16,4,8,32]{4,1,3,2,0:T(8,128)}, f32[16,16,4,8,32]{4,1,3,2,0:T(8,128)S(1)}, u32[]{:S(2)}) copy-start(f32[16,16,4,8,32]{4,1,3,2,0:T(8,128)S(1)} %get-tuple-element.11) | copy-start | bytes 3145732
  73.3 7.3 %copy-start.2 = (bf16[16,16,256]{2,1,0:T(8,128)(2,1)S(1)}, bf16[16,16,256]{2,1,0:T(8,128)(2,1)}, u32[]{:S(2)}) copy-start(bf16[16,16,256]{2,1,0:T(8,128)(2,1)} %param.10) | copy-start | bytes 393220
  81.8 8.9 %copy-start.3 = (bf16[256,256]{1,0:T(8,128)(2,1)}, bf16[256,256]{1,0:T(8,128)(2,1)S(1)}, u32[]{:S(2)}) copy-start(bf16[256,256]{1,0:T(8,128)(2,1)S(1)} %get-tuple-element.13) | copy-start | bytes 393220
  97.3 7.6 %copy-start.6 = (bf16[16,16]{0,1:T(8,128)(2,1)S(1)}, bf16[16,16]{0,1:T(8,128)(2,1)}, u32[]{:S(2)}) copy-start(bf16[16,16]{0,1:T(8,128)(2,1)} %copy-done.5) | copy-start | bytes 1540
  97.3 29.4 %copy-start.4 = (bf16[16,16,128]{2,1,0:T(8,128)(2,1)S(1)}, bf16[16,16,128]{2,1,0:T(8,128)(2,1)}, u32[]{:S(2)}) copy-start(bf16[16,16,128]{2,1,0:T(8,128)(2,1)} %param.11) | copy-start | bytes 196612
Sparse Core Ops, SparseCore 0:
  105.0 21.6 reduce-scatter.1
where the time goes:
time: 136 us; the launch traced here: 135 us
  blocking collectives  69.9 us (51%)
  matrix products  21.6 us (16%)
  between operations  14.3 us (11%)
  local copies, waits for them, and re-layouts  11.6 us (9%)
  waiting for transfers between devices  9.57 us (7%)
  other arithmetic  8.21 us (6%)
    all_gather x1, blocking collectives, shards(): lax.all_gather(value_rows, 'res', axis=1, tiled=True)  15.8 us
    all_gather x1, blocking collectives, shards(): lax.all_gather(key_rows, 'res', axis=1, tiled=True)  15.7 us
    all_gather x1, blocking collectives, shards(): full_bias = lax.all_gather(local_bias, 'seq', axis=1, tiled=True)  14 us
    psum x1, blocking collectives, shards(): count_sum = lax.psum(own_counts, 'seq')  12.1 us
    reduce_scatter x1, waiting for transfers between devices, shards(): lax.psum_scatter(jnp.dot(block, proj_wide, precision=lax.Precision.HIGHES...  9.56 us
    dot_general x1, matrix products, shards(): jnp.dot(block, proj_wide, precision=lax.Precision.HIGHEST)  7.53 us
    transpose x1, local copies, waits for them, and re-layouts, shards(): jnp.einsum('sip,sjq->jipq', left, all_right, preferred_element_type=jnp.f...  6.49 us
    all_gather x1, blocking collectives, shards(): lax.all_gather(valid_entries, 'res', axis=1, tiled=True)  6.17 us
  transfers between devices with their start and end apart: 1, of which 1 were waited for; matrix products, arithmetic and copies ran while one was open for 0% of the time, Pallas kernels for 0%

commit v1 on v0

v1 whole, which is shorter than its diff:
```python
import functools
import math

import jax
import jax.numpy as jnp
from jax import lax
from jax.experimental import pallas as pl
from jax.experimental.pallas import tpu as pltpu
from jax.sharding import PartitionSpec as P

MESH = pl.DeviceIdType.MESH
F32 = jnp.float32
BF16 = jnp.bfloat16


def iota(shape, dim):
    return lax.broadcasted_iota(jnp.int32, shape, dim)


def standardize(values):
    center = jnp.mean(values, axis=-1, keepdims=True)
    shifted = values - center
    spread = jnp.mean(shifted * shifted, axis=-1, keepdims=True)
    return shifted * lax.rsqrt(spread + 1e-05)


def dot(a, b, dims=((1,), (0,)), precision=None):
    return lax.dot_general(a, b, (dims, ((), ())), precision=precision, preferred_element_type=F32)


def indicator(condition):
    return jnp.where(condition, 1.0, 0.0).astype(BF16)


def kernel(
    Z,
    R,
    x_hbm,
    edge_ref,
    homolog_ref,
    amino_ref,
    stretch_ref,
    qkvg_hbm,
    logit_ref,
    blend_hbm,
    operand_ref,
    product_hbm,
    y_hbm,
    pair_ref,
    xall,
    qkvg,
    blend,
    product,
    notes,
    usable,
    bias,
    ybuf,
    lbuf,
    rbuf,
    gbuf,
    grouped,
    unfolded,
    local_sem,
    x_send,
    x_recv,
    n_send,
    n_recv,
    y_send,
    y_recv,
    g_send,
    g_recv,
):
    N, I, W = x_hbm.shape
    C, E = edge_ref.shape[1:]
    H = logit_ref.shape[1]
    DH = blend_hbm.shape[0] // H
    Q = operand_ref.shape[1] // 2
    S = N // R
    L = R * I
    D = R * Z
    T = S * L
    G = 128 // Q
    PH = Q // G
    GB = max(1, I * C // 128)
    IG = I // GB

    part = lax.axis_index("parts")
    z = lax.axis_index("seq")
    r = lax.axis_index("res")
    me = r * Z + z

    loads = [
        pltpu.make_async_copy(x_hbm.at[pl.ds(r * S, S)], xall.at[r], local_sem.at[0]),
        pltpu.make_async_copy(qkvg_hbm, qkvg, local_sem.at[1]),
        pltpu.make_async_copy(blend_hbm, blend, local_sem.at[2]),
        pltpu.make_async_copy(product_hbm, product, local_sem.at[3]),
    ]
    for load in loads:
        load.start()

    def peer(k):
        other = lax.rem(me + k, D)
        return other // Z, lax.rem(other, Z)

    barrier = pltpu.get_barrier_semaphore()

    def greet(k, carry):
        pr, pz = peer(k)
        pl.semaphore_signal(barrier, inc=1, device_id=(part, pz, pr), device_id_type=MESH)
        return carry

    lax.fori_loop(1, D, greet, 0)
    pl.semaphore_wait(barrier, D - 1)

    def x_copy(k):
        pr = lax.rem(r + k, R)
        return pltpu.make_async_remote_copy(
            src_ref=x_hbm.at[pl.ds(pr * S, S)],
            dst_ref=xall.at[r],
            send_sem=x_send,
            recv_sem=x_recv,
            device_id=(part, z, pr),
            device_id_type=MESH,
        )

    for k in range(1, R):
        x_copy(k).start()

    edge = edge_ref[...].astype(F32).reshape(I * C, E)
    bias_rows = dot(
        jnp.transpose(logit_ref[...]), standardize(edge), ((1,), (1,)), lax.Precision.HIGHEST
    )
    width = IG * C
    pieces = [bias_rows[:, g * width : (g + 1) * width] for g in range(GB)]
    bias_rows = jnp.concatenate(pieces, axis=0) if GB > 1 else pieces[0]
    bias_rows = jnp.pad(bias_rows, ((0, 16 - GB * H), (0, 128 - width)))
    valid = (homolog_ref[...] * amino_ref[...][None, :]).astype(F32)
    notes[me, :, 0:128] = bias_rows.astype(BF16)
    notes[me, :, 128:256] = jnp.pad(valid, ((0, 0), (0, 128 - I))).astype(BF16)

    def send_notes(k, carry):
        pr, pz = peer(k)
        pltpu.make_async_remote_copy(
            src_ref=notes.at[me],
            dst_ref=notes.at[me],
            send_sem=n_send,
            recv_sem=n_recv,
            device_id=(part, pz, pr),
            device_id_type=MESH,
        ).start()
        return carry

    lax.fori_loop(1, D, send_notes, 0)

    lane = iota((2 * Q, 128), 1)
    channel = iota((2 * Q, 128), 0)
    spread_left = [indicator(channel == lax.rem(lane, PH) * G + g) for g in range(G)]
    spread_right = indicator(channel == Q + lax.rem(lane, Q))
    spread = jnp.concatenate(spread_left + [spread_right], axis=1)
    operand = dot(operand_ref[...], spread).astype(BF16)

    def all_but_one(ref, sem):
        window = ref.at[pl.ds(0, ref.shape[0] - 1)]
        return pltpu.make_async_copy(window, window, sem)

    loads[0].wait()
    loads[1].wait()
    all_but_one(xall, x_recv).wait()
    x = jnp.concatenate(
        [xall[rr, s] for s in range(S) for rr in range(R)], axis=0
    ).astype(F32)
    normed = (standardize(x) * stretch_ref[...][None, :]).astype(BF16)
    HW = H * DH
    queries = (dot(normed, qkvg[:, 0:HW]) * (1.0 / math.sqrt(DH))).astype(BF16)
    keys = dot(normed, qkvg[:, HW : 2 * HW]).astype(BF16)
    values = dot(normed, qkvg[:, 2 * HW : 3 * HW]).astype(BF16)
    gating = jax.nn.sigmoid(dot(normed, qkvg[:, 3 * HW : 4 * HW]))

    head_of_lane = iota((1, HW), 1) // DH
    head_masks = [indicator(head_of_lane == h) for h in range(H)]

    def raw_scores(s):
        q = queries[s * L : (s + 1) * L]
        expanded = jnp.concatenate([q * head_masks[h] for h in range(H)], axis=0)
        return dot(expanded, keys[s * L : (s + 1) * L], ((1,), (1,)))

    all_but_one(notes, n_recv).wait()
    KZ = Z * 128
    row = iota((KZ, L), 0)
    fold = indicator(
        ((row % 128) % C + (row // 128) * C == iota((KZ, L), 1)) & (row % 128 < width)
    )
    own_lane = jnp.where((iota((IG, KZ), 1) % 128) // C == iota((IG, KZ), 0), 1.0, 0.0)
    for rr in range(R):
        wide = jnp.concatenate(
            [notes[rr * Z + zz, :, 0:128] for zz in range(Z)], axis=1
        ).astype(F32)[: GB * H]
        wide = (wide[:, None, :] * own_lane[None]).reshape(GB * H * IG, KZ).astype(BF16)
        block = dot(wide, fold).reshape(GB, H, IG, L)
        for g in range(GB):
            bias[:, pl.ds(rr * I + g * IG, IG), :] = block[g]

    mask_rows = jnp.concatenate([notes[rr * Z + z, :, 128:256] for rr in range(R)], axis=1)
    prow = iota((R * 128, L), 0)
    place = indicator(
        (prow % 128 + (prow // 128) * I == iota((R * 128, L), 1)) & (prow % 128 < I)
    )
    usable[...] = dot(mask_rows, place)
    usable_rows = [usable[pl.ds(r * S + s, 1), :] for s in range(S)]
    pair_bias = bias[...].reshape(H * L, L)

    attended = []
    for s in range(S):
        scores = raw_scores(s) + pair_bias
        scores = jnp.where(usable_rows[s] > 0, scores, -1000000000.0)
        raised = jnp.exp(scores - jnp.max(scores, axis=-1, keepdims=True))
        weights = (raised * (1.0 / jnp.sum(raised, axis=-1, keepdims=True))).astype(BF16)
        mixed = dot(weights, values[s * L : (s + 1) * L])
        total = mixed[0:L] * head_masks[0].astype(F32)
        for h in range(1, H):
            total = total + mixed[h * L : (h + 1) * L] * head_masks[h].astype(F32)
        attended.append(total.astype(BF16))
    attended = jnp.concatenate(attended, axis=0).astype(F32)
    gated = (gating * attended).astype(BF16)
    loads[2].wait()
    stack = (x + dot(gated, blend[...])).astype(BF16)
    for s in range(S):
        for rr in range(R):
            start = s * L + rr * I
            ybuf[rr, s] = stack[start : start + I]

    def y_copy(k):
        pr = lax.rem(r + k, R)
        return pltpu.make_async_remote_copy(
            src_ref=ybuf.at[pr],
            dst_ref=y_hbm.at[pl.ds(r * S, S)],
            send_sem=y_send,
            recv_sem=y_recv,
            device_id=(part, z, pr),
            device_id_type=MESH,
        )

    outer_normed = standardize(stack.astype(F32)).astype(BF16)
    factors = dot(outer_normed, operand)
    diagonal = iota((L, L), 0) == iota((L, L), 1)
    valid_column = jnp.concatenate(
        [
            jnp.sum(jnp.where(diagonal, usable_rows[s], 0.0), axis=1, keepdims=True)
            for s in range(S)
        ],
        axis=0,
    )
    residue = iota((T, 128), 0) % I
    tile_lane = iota((T, 128), 1)
    left_mask = jnp.where(tile_lane // PH == residue, valid_column, 0.0)
    JL = 128 // Q
    stacked = []
    for g in range(G):
        left = factors[:, g * 128 : (g + 1) * 128] * left_mask
        right = factors[:, G * 128 : (G + 1) * 128] * jnp.where(
            tile_lane // Q + g * JL == residue, valid_column, 0.0
        )
        stacked.append(jnp.concatenate([left, right], axis=1).astype(BF16))
    stacked = jnp.concatenate(stacked, axis=0)
    out_row = iota((R * 16, G * T), 0)
    in_row = iota((R * 16, G * T), 1)
    in_code = (in_row % L) // I * 16 + (in_row // T) * S + (in_row % T) // L
    message = dot(indicator(out_row == in_code), stacked).astype(BF16)
    message = message.reshape(R, 16, 256)
    lbuf[...] = message[:, :, 0:128]
    rbuf[...] = message[:, :, 128:256]

    def g_copies(k):
        pr, pz = peer(k)
        both = []
        for source, first in ((lbuf.at[pr], 0), (rbuf.at[pz * C // I], 128)):
            both.append(
                pltpu.make_async_remote_copy(
                    src_ref=source,
                    dst_ref=gbuf.at[me, :, pl.ds(first, 128)],
                    send_sem=g_send,
                    recv_sem=g_recv,
                    device_id=(part, pz, pr),
                    device_id_type=MESH,
                )
            )
        return both

    def send_factors(k, carry):
        for copy in g_copies(k):
            copy.start()
        return carry

    lax.fori_loop(1, D, send_factors, 0)
    own_out = pltpu.make_async_copy(ybuf.at[r], y_hbm.at[pl.ds(r * S, S)], local_sem.at[0])
    own_out.start()
    for k in range(1, R):
        y_copy(k).start()
    block_of_columns = z * C // I
    gbuf[me, :, 0:128] = lbuf[r]
    gbuf[me, :, 128:256] = rbuf[block_of_columns]

    rows_i = jnp.concatenate([notes[r * Z + zz, :, 128:256] for zz in range(Z)], axis=0)
    rows_j = jnp.concatenate(
        [notes[block_of_columns * Z + zz, :, 128:256] for zz in range(Z)], axis=0
    )
    counts = dot(rows_i, rows_j, ((0,), (0,)))[:I]
    first_column = lax.rem(z * C, I)
    pick = iota((C, 128), 1) == iota((C, 128), 0) + first_column
    counts = jnp.sum(jnp.where(pick[None], counts[:, None, :], 0.0), axis=-1, keepdims=True)
    inverse = 1.0 / jnp.maximum(counts, 1.0)

    SD = 16 * S
    srow = iota((G * SD, 256), 0)
    code = (srow // S) % 16 * 16 + (srow // SD) * S + srow % S
    regroup = indicator(code == iota((G * SD, 256), 1))
    NJ = C // JL
    loads[3].wait()
    all_but_one(gbuf, g_recv).wait()
    outer = [0.0] * G
    for chunk in range(D // 16):
        rows = gbuf[chunk * 16 : (chunk + 1) * 16].reshape(256, 256)
        ordered = dot(regroup, rows)
        if C == I:
            right = [ordered[t * SD : (t + 1) * SD, 128:256] for t in range(NJ)]
        else:
            grouped[...] = ordered
            first = pl.multiple_of(first_column // JL * SD, 8)
            right = [grouped[pl.ds(first + t * SD, SD), 128:256] for t in range(NJ)]
        right = jnp.concatenate(right, axis=1).astype(BF16)
        for g in range(G):
            left = ordered[g * SD : (g + 1) * SD, 0:128].astype(BF16)
            outer[g] = outer[g] + dot(left, right, ((0,), (0,)))
    low_half = iota((1, 128), 1) < 64
    even = (iota((1, 128), 1) // 32) % 2 == 0
    for t in range(NJ):
        tiles = [outer[g][:, t * 128 : (t + 1) * 128] for g in range(G)]
        for g in (0, 1):
            a, b = tiles[g], tiles[g + 2]
            tiles[g] = jnp.where(low_half, a, pltpu.roll(b, 64, 1))
            tiles[g + 2] = jnp.where(low_half, pltpu.roll(a, 64, 1), b)
        for g in (0, 2):
            a, b = tiles[g], tiles[g + 1]
            tiles[g] = jnp.where(even, a, pltpu.roll(b, 32, 1))
            tiles[g + 1] = jnp.where(even, pltpu.roll(a, 96, 1), b)
        for g in range(JL):
            for i in range(I):
                unfolded[pl.ds((i * C + t * JL + g) * PH, PH), :] = tiles[g][i * PH : (i + 1) * PH]
    couples = jnp.concatenate(
        [unfolded[pl.ds(p, I * C, stride=PH), :] for p in range(PH)], axis=1
    )
    high = couples.astype(BF16)
    low = (couples - high.astype(F32)).astype(BF16)
    update = dot(high, product[...]) + dot(low, product[...])
    pair = edge_ref[...].astype(F32) + update.reshape(I, C, E) * inverse
    pair_ref[...] = pair.astype(BF16)

    own_out.wait()
    all_but_one(ybuf, y_recv).wait()
    all_but_one(xall, x_send).wait()
    all_but_one(ybuf, y_send).wait()
    all_but_one(notes, n_send).wait()
    all_but_one(gbuf, g_send).wait()


def shards(x, edge, homolog, amino, stretch, qkvg, logit, blend, operand, product):
    Z, R = lax.axis_size("seq"), lax.axis_size("res")
    N, I, W = x.shape
    C, E = edge.shape[1:]
    H = logit.shape[1]
    S, L, D = N // R, R * I, R * Z
    vmem = pl.BlockSpec(memory_space=pltpu.VMEM)
    hbm = pl.BlockSpec(memory_space=pl.ANY)
    dma = pltpu.SemaphoreType.DMA
    return pl.pallas_call(
        functools.partial(kernel, Z, R),
        out_shape=(
            jax.ShapeDtypeStruct(x.shape, BF16),
            jax.ShapeDtypeStruct(edge.shape, BF16),
        ),
        in_specs=[hbm, vmem, vmem, vmem, vmem, hbm, vmem, hbm, vmem, hbm],
        out_specs=(hbm, vmem),
        scratch_shapes=[
            pltpu.VMEM((R, S, I, W), BF16),
            pltpu.VMEM(qkvg.shape, BF16),
            pltpu.VMEM(blend.shape, BF16),
            pltpu.VMEM(product.shape, BF16),
            pltpu.VMEM((D, 16, 256), BF16),
            pltpu.VMEM((N, L), F32),
            pltpu.VMEM((H, L, L), F32),
            pltpu.VMEM((R, S, I, W), BF16),
            pltpu.VMEM((R, 16, 128), BF16),
            pltpu.VMEM((R, 16, 128), BF16),
            pltpu.VMEM((D, 16, 256), BF16),
            pltpu.VMEM((4 * 16 * S, 256), F32),
            pltpu.VMEM((I * C * 8, 128), F32),
            dma((4,)),
            dma,
            dma,
            dma,
            dma,
            dma,
            dma,
            dma,
            dma,
        ],
        compiler_params=pltpu.CompilerParams(
            collective_id=0, has_side_effects=True, vmem_limit_bytes=48 * 1024 * 1024
        ),
        cost_estimate=pl.CostEstimate(
            flops=400_000_000, bytes_accessed=1_500_000, transcendentals=200_000
        ),
    )(x, edge, homolog, amino, stretch, qkvg, logit, blend, operand, product)


def solution(mesh):
    in_specs = (
        P(("parts", "seq"), "res", None),
        P(("parts", "res"), "seq", None),
        P(("parts", "seq"), "res"),
        P(("parts", "res")),
        P(),
        P(),
        P(),
        P(),
        P(),
        P(),
    )
    out_specs = (P(("parts", "seq"), "res", None), P(("parts", "res"), "seq", None))
    return jax.shard_map(shards, mesh=mesh, in_specs=in_specs, out_specs=out_specs, check_vma=False)
```

time: 136 us -> 28.4 us (0.21)
  blocking collectives: 69.9 us -> 0 us
  matrix products: 21.6 us -> 0 us
  Pallas kernels: 0 us -> 20.6 us
  between operations: 14.3 us -> 0.71 us
  waiting for transfers between devices: 9.57 us -> 0 us
  other arithmetic: 8.21 us -> 0 us
  local copies, waits for them, and re-layouts: 11.6 us -> 6.75 us
    all_gather x5 -> x0, blocking collectives: 57.8 us -> none  [the longest x1 15.8 us: shards(): lax.all_gather(value_rows, 'res', axis=1, tiled=True)]
    dot_general x9 -> x0, matrix products: 21.6 us -> none  [the longest x1 7.53 us: shards(): jnp.dot(block, proj_wide, precision=lax.Precision.HIGHEST)]
    pallas_call x0 -> x1, Pallas kernels: none -> 20.6 us  [shards(): pl.pallas_call(functools.partial(kernel, Z, R), out_shape=(jax.ShapeDtype...]
    psum x1 -> x0, blocking collectives: 12.1 us -> none  [shards(): count_sum = lax.psum(own_counts, 'seq')]
    reduce_scatter x1 -> x0, waiting for transfers between devices: 9.56 us -> none  [shards(): lax.psum_scatter(jnp.dot(block, proj_wide, precision=lax.Precision.HIGHES...]
    transpose x2 -> x0, local copies, waits for them, and re-layouts: 6.61 us -> none  [the longest x1 6.49 us: shards(): jnp.einsum('sip,sjq->jipq', left, all_right, preferred_element_type=jnp.f...]
    unnamed x16 -> x20, local copies, waits for them, and re-layouts: 2.1 us -> 6.75 us
    reduce_sum x5 -> x0, other arithmetic: 4.25 us -> none  [the longest x3 2.3 us: standardize_features(): spread = jnp.mean(shifted * shifted, axis=-1, keepdims=True)]
  transfers between devices with their start and end apart: 1 -> 0, of which waited for: 1 -> 0; matrix products, arithmetic and copies ran while one was open for 0% -> 0% of each run, Pallas kernels for 0% -> 0%
where the time goes in v1:
time: 28.4 us; the launch traced here: 28 us
  Pallas kernels  20.6 us (73%)
  local copies, waits for them, and re-layouts  6.75 us (24%)
  between operations  0.71 us (2%)
    pallas_call x1, Pallas kernels, shards(): pl.pallas_call(functools.partial(kernel, Z, R), out_shape=(jax.ShapeDtype...  20.6 us
    unnamed x20, local copies, waits for them, and re-layouts  6.75 us

profile of v1, /device:TPU:0, one launch (start us, length us, event | category | flops | bytes accessed | tf_op | source)
XLA Modules:
  0.0 28.0 jit_solution(5948802521854711805)
XLA Ops:
  0.6 0.0 copy-start.2
  0.6 0.8 %copy.12.logit_ref = f32[128,8]{1,0:T(8,128)S(1)} copy(f32[128,8]{0,1:T(8,128)} %param.16) | data formatting | bytes 8192 | tf_op args[6]
  1.5 0.0 copy-start.5
  1.5 0.0 copy-start.6
  1.5 0.0 copy-start.7
  1.5 0.9 %copy.13.operand_ref = bf16[256,64]{1,0:T(8,128)(2,1)S(1)} copy(bf16[256,64]{0,1:T(8,128)(2,1)} %param.18) | data formatting | bytes 65536 | tf_op args[8]
  2.4 0.0 copy-done.2
  2.4 0.0 copy-done.5
  2.4 0.0 copy-done.6
  2.4 0.0 copy-done.7
  2.4 0.0 copy-start
  2.4 1.0 %copy-done = bf16[256,1024]{1,0:T(8,128)(2,1)S(1)} copy-done((bf16[256,1024]{1,0:T(8,128)(2,1)S(1)}, bf16[256,1024]{1,0:T(8,128)(2,1)}, u32[]{:S(2)}) %copy-start) | copy-done | bytes 524312
  3.5 0.0 copy-start.1
  3.5 0.9 %copy-done.1 = bf16[1024,128]{1,0:T(8,128)(2,1)S(1)} copy-done((bf16[1024,128]{1,0:T(8,128)(2,1)S(1)}, bf16[1024,128]{1,0:T(8,128)(2,1)}, u32[]{:S(2)}) %copy-start.1) | copy-done | bytes 262168
  4.4 0.0 copy-start.3
  4.4 0.9 %copy-done.3 = bf16[256,256]{1,0:T(8,128)(2,1)S(1)} copy-done((bf16[256,256]{1,0:T(8,128)(2,1)S(1)}, bf16[256,256]{1,0:T(8,128)(2,1)}, u32[]{:S(2)}) %copy-start.3) | copy-done | bytes 131096
  5.3 0.0 copy-start.4
  5.3 0.8 %copy-done.4 = bf16[16,16,128]{2,1,0:T(8,128)(2,1)S(1)} copy-done((bf16[16,16,128]{2,1,0:T(8,128)(2,1)S(1)}, bf16[16,16,128]{2,1,0:T(8,128)(2,1)}, u32[]{:S(2)}) %copy-start.4) | copy-done | bytes 65560
  6.2 20.6 %shard_map.113 = (bf16[16,16,256]{2,1,0:T(8,128)(2,1)S(1)}, bf16[16,16,128]{2,1,0:T(8,128)(2,1)S(1)}) custom-call(bf16[16,16,256]{2,1,0:T(8,128)(2,1)S(1)} %copy-done.2, bf16[16,16,128]{2,1,0:T(8,128)(2,1)S(1)} %copy-done.4, s32[16,16]{1,0:T(8,128)S(1)} %copy-done.5, s32[16]{0:T(128)S(1)} %copy-done.7, f32[256]{0:T(256)S(1)} %copy-done.6, ...), custom_call_target="tpu_custom_call" | custom-call | flops 400000000 | bytes 1500000 | tf_op jit(solution)/shard_map/pallas_call | solution.py:375
  26.8 0.7 %copy.16 = bf16[16,16,256]{2,1,0:T(8,128)(2,1)} copy(bf16[16,16,256]{2,1,0:T(8,128)(2,1)S(1)} %get-tuple-element.4) | data formatting | bytes 262144
  27.4 0.6 %copy.17 = bf16[16,16,128]{2,1,0:T(8,128)(2,1)} copy(bf16[16,16,128]{2,1,0:T(8,128)(2,1)S(1)} %get-tuple-element.5) | data formatting | bytes 131072
Async XLA Ops:
  0.6 1.8 %copy-start.2 = (bf16[16,16,256]{2,1,0:T(8,128)(2,1)S(1)}, bf16[16,16,256]{2,1,0:T(8,128)(2,1)}, u32[]{:S(2)}) copy-start(bf16[16,16,256]{2,1,0:T(8,128)(2,1)} %x_hbm.1) | copy-start | bytes 393220
  1.5 0.9 %copy-start.5 = (s32[16,16]{1,0:T(8,128)S(1)}, s32[16,16]{1,0:T(8,128)}, u32[]{:S(2)}) copy-start(s32[16,16]{1,0:T(8,128)} %homolog_ref.1) | copy-start | bytes 3076
  1.5 0.9 %copy-start.6 = (f32[256]{0:T(256)S(1)}, f32[256]{0:T(256)}, u32[]{:S(2)}) copy-start(f32[256]{0:T(256)} %stretch_ref.1) | copy-start | bytes 3076
  1.5 0.9 %copy-start.7 = (s32[16]{0:T(128)S(1)}, s32[16]{0:T(128)}, u32[]{:S(2)}) copy-start(s32[16]{0:T(128)} %amino_ref.1) | copy-start | bytes 196
  2.4 1.0 %copy-start = (bf16[256,1024]{1,0:T(8,128)(2,1)S(1)}, bf16[256,1024]{1,0:T(8,128)(2,1)}, u32[]{:S(2)}) copy-start(bf16[256,1024]{1,0:T(8,128)(2,1)} %qkvg_hbm.1) | copy-start | bytes 1572868
  3.5 0.9 %copy-start.1 = (bf16[1024,128]{1,0:T(8,128)(2,1)S(1)}, bf16[1024,128]{1,0:T(8,128)(2,1)}, u32[]{:S(2)}) copy-start(bf16[1024,128]{1,0:T(8,128)(2,1)} %product_hbm.1) | copy-start | bytes 786436
  4.4 0.9 %copy-start.3 = (bf16[256,256]{1,0:T(8,128)(2,1)S(1)}, bf16[256,256]{1,0:T(8,128)(2,1)}, u32[]{:S(2)}) copy-start(bf16[256,256]{1,0:T(8,128)(2,1)} %blend_hbm.1) | copy-start | bytes 393220
  5.3 0.8 %copy-start.4 = (bf16[16,16,128]{2,1,0:T(8,128)(2,1)S(1)}, bf16[16,16,128]{2,1,0:T(8,128)(2,1)}, u32[]{:S(2)}) copy-start(bf16[16,16,128]{2,1,0:T(8,128)(2,1)} %edge_ref.1) | copy-start | bytes 196612

commit v2 on v1

--- a/solution.py
+++ b/solution.py
@@ -36,18 +36,24 @@
     Z,
     R,
     x_hbm,
+    edge_hbm,
+    homolog_hbm,
+    amino_hbm,
+    stretch_hbm,
+    qkvg_hbm,
+    logit_hbm,
+    blend_hbm,
+    operand_hbm,
+    product_hbm,
+    y_hbm,
+    pair_ref,
+    xall,
     edge_ref,
     homolog_ref,
     amino_ref,
     stretch_ref,
-    qkvg_hbm,
     logit_ref,
-    blend_hbm,
     operand_ref,
-    product_hbm,
-    y_hbm,
-    pair_ref,
-    xall,
     qkvg,
     blend,
     product,
@@ -71,10 +77,10 @@
     g_recv,
 ):
     N, I, W = x_hbm.shape
-    C, E = edge_ref.shape[1:]
-    H = logit_ref.shape[1]
+    C, E = edge_hbm.shape[1:]
+    H = logit_hbm.shape[0]
     DH = blend_hbm.shape[0] // H
-    Q = operand_ref.shape[1] // 2
+    Q = operand_hbm.shape[0] // 2
     S = N // R
     L = R * I
     D = R * Z
@@ -89,27 +95,56 @@
     r = lax.axis_index("res")
     me = r * Z + z
 
+    def peer(k):
+        other = lax.rem(me + k, D)
+        return other // Z, lax.rem(other, Z)
+
+    barrier = pltpu.get_barrier_semaphore()
+
+    def greet(k, carry):
+        pr, pz = peer(k)
+        pl.semaphore_signal(barrier, inc=1, device_id=(part, pz, pr), device_id_type=MESH)
+        return carry
+
+    lax.fori_loop(1, D, greet, 0)
+
     loads = [
         pltpu.make_async_copy(x_hbm.at[pl.ds(r * S, S)], xall.at[r], local_sem.at[0]),
         pltpu.make_async_copy(qkvg_hbm, qkvg, local_sem.at[1]),
         pltpu.make_async_copy(blend_hbm, blend, local_sem.at[2]),
         pltpu.make_async_copy(product_hbm, product, local_sem.at[3]),
+        pltpu.make_async_copy(edge_hbm, edge_ref, local_sem.at[4]),
+        pltpu.make_async_copy(logit_hbm, logit_ref, local_sem.at[5]),
+        pltpu.make_async_copy(homolog_hbm, homolog_ref, local_sem.at[6]),
+        pltpu.make_async_copy(amino_hbm, amino_ref, local_sem.at[7]),
+        pltpu.make_async_copy(operand_hbm, operand_ref, local_sem.at[8]),
+        pltpu.make_async_copy(stretch_hbm, stretch_ref, local_sem.at[9]),
     ]
-    for load in loads:
+    for load in loads[4:] + loads[:4]:
         load.start()
 
-    def peer(k):
-        other = lax.rem(me + k, D)
-        return other // Z, lax.rem(other, Z)
-
-    barrier = pltpu.get_barrier_semaphore()
-
-    def greet(k, carry):
-        pr, pz = peer(k)
-        pl.semaphore_signal(barrier, inc=1, device_id=(part, pz, pr), device_id_type=MESH)
-        return carry
-
-    lax.fori_loop(1, D, greet, 0)
+    for load in loads[4:8]:
+        load.wait()
+    edge = edge_ref[...].astype(F32).reshape(I * C, E)
+    bias_rows = dot(
+        logit_ref[...], standardize(edge), ((1,), (1,)), lax.Precision.HIGHEST
+    )
+    width = IG * C
+    pieces = [bias_rows[:, g * width : (g + 1) * width] for g in range(GB)]
+    bias_rows = jnp.concatenate(pieces, axis=0) if GB > 1 else pieces[0]
+    bias_rows = jnp.pad(bias_rows, ((0, 16 - GB * H), (0, 128 - width)))
+    valid = (homolog_ref[...] * amino_ref[...][None, :]).astype(F32)
+    notes[me, :, 0:128] = bias_rows.astype(BF16)
+    notes[me, :, 128:256] = jnp.pad(valid, ((0, 0), (0, 128 - I))).astype(BF16)
+
+    lane = iota((2 * Q, 128), 1)
+    channel = iota((2 * Q, 128), 0)
+    spread_left = [indicator(channel == lax.rem(lane, PH) * G + g) for g in range(G)]
+    spread_right = indicator(channel == Q + lax.rem(lane, Q))
+    spread = jnp.concatenate(spread_left + [spread_right], axis=1)
+    loads[8].wait()
+    operand = dot(operand_ref[...], spread, ((0,), (0,))).astype(BF16)
+
     pl.semaphore_wait(barrier, D - 1)
 
     def x_copy(k):
@@ -122,21 +157,6 @@
             device_id=(part, z, pr),
             device_id_type=MESH,
         )
-
-    for k in range(1, R):
-        x_copy(k).start()
-
-    edge = edge_ref[...].astype(F32).reshape(I * C, E)
-    bias_rows = dot(
-        jnp.transpose(logit_ref[...]), standardize(edge), ((1,), (1,)), lax.Precision.HIGHEST
-    )
-    width = IG * C
-    pieces = [bias_rows[:, g * width : (g + 1) * width] for g in range(GB)]
-    bias_rows = jnp.concatenate(pieces, axis=0) if GB > 1 else pieces[0]
-    bias_rows = jnp.pad(bias_rows, ((0, 16 - GB * H), (0, 128 - width)))
-    valid = (homolog_ref[...] * amino_ref[...][None, :]).astype(F32)
-    notes[me, :, 0:128] = bias_rows.astype(BF16)
-    notes[me, :, 128:256] = jnp.pad(valid, ((0, 0), (0, 128 - I))).astype(BF16)
 
     def send_notes(k, carry):
         pr, pz = peer(k)
@@ -151,13 +171,8 @@
         return carry
 
     lax.fori_loop(1, D, send_notes, 0)
-
-    lane = iota((2 * Q, 128), 1)
-    channel = iota((2 * Q, 128), 0)
-    spread_left = [indicator(channel == lax.rem(lane, PH) * G + g) for g in range(G)]
-    spread_right = indicator(channel == Q + lax.rem(lane, Q))
-    spread = jnp.concatenate(spread_left + [spread_right], axis=1)
-    operand = dot(operand_ref[...], spread).astype(BF16)
+    for k in range(1, R):
+        x_copy(k).start()
 
     def all_but_one(ref, sem):
         window = ref.at[pl.ds(0, ref.shape[0] - 1)]
@@ -165,6 +180,7 @@
 
     loads[0].wait()
     loads[1].wait()
+    loads[9].wait()
     all_but_one(xall, x_recv).wait()
     x = jnp.concatenate(
         [xall[rr, s] for s in range(S) for rr in range(R)], axis=0
@@ -184,6 +200,8 @@
         expanded = jnp.concatenate([q * head_masks[h] for h in range(H)], axis=0)
         return dot(expanded, keys[s * L : (s + 1) * L], ((1,), (1,)))
 
+    raw = [raw_scores(s) for s in range(S)]
+
     all_but_one(notes, n_recv).wait()
     KZ = Z * 128
     row = iota((KZ, L), 0)
@@ -211,7 +229,7 @@
 
     attended = []
     for s in range(S):
-        scores = raw_scores(s) + pair_bias
+        scores = raw[s] + pair_bias
         scores = jnp.where(usable_rows[s] > 0, scores, -1000000000.0)
         raised = jnp.exp(scores - jnp.max(scores, axis=-1, keepdims=True))
         weights = (raised * (1.0 / jnp.sum(raised, axis=-1, keepdims=True))).astype(BF16)
@@ -364,13 +382,14 @@
 
 
 def shards(x, edge, homolog, amino, stretch, qkvg, logit, blend, operand, product):
+    logit, operand = logit.T, operand.T
     Z, R = lax.axis_size("seq"), lax.axis_size("res")
     N, I, W = x.shape
     C, E = edge.shape[1:]
-    H = logit.shape[1]
+    H = logit.shape[0]
     S, L, D = N // R, R * I, R * Z
     vmem = pl.BlockSpec(memory_space=pltpu.VMEM)
-    hbm = pl.BlockSpec(memory_space=pl.ANY)
+    hbm = pl.BlockSpec(memory_space=pltpu.HBM)
     dma = pltpu.SemaphoreType.DMA
     return pl.pallas_call(
         functools.partial(kernel, Z, R),
@@ -378,10 +397,16 @@
             jax.ShapeDtypeStruct(x.shape, BF16),
             jax.ShapeDtypeStruct(edge.shape, BF16),
         ),
-        in_specs=[hbm, vmem, vmem, vmem, vmem, hbm, vmem, hbm, vmem, hbm],
+        in_specs=[hbm] * 10,
         out_specs=(hbm, vmem),
         scratch_shapes=[
             pltpu.VMEM((R, S, I, W), BF16),
+            pltpu.VMEM(edge.shape, BF16),
+            pltpu.VMEM(homolog.shape, jnp.int32),
+            pltpu.VMEM(amino.shape, jnp.int32),
+            pltpu.VMEM(stretch.shape, F32),
+            pltpu.VMEM(logit.shape, F32),
+            pltpu.VMEM(operand.shape, BF16),
             pltpu.VMEM(qkvg.shape, BF16),
             pltpu.VMEM(blend.shape, BF16),
             pltpu.VMEM(product.shape, BF16),
@@ -394,7 +419,7 @@
             pltpu.VMEM((D, 16, 256), BF16),
             pltpu.VMEM((4 * 16 * S, 256), F32),
             pltpu.VMEM((I * C * 8, 128), F32),
-            dma((4,)),
+            dma((10,)),
             dma,
             dma,
             dma,
@@ -405,7 +430,7 @@
             dma,
         ],
         compiler_params=pltpu.CompilerParams(
-            collective_id=0, has_side_effects=True, vmem_limit_bytes=48 * 1024 * 1024
+            collective_id=0, has_side_effects=True, vmem_limit_bytes=64 * 1024 * 1024
         ),
         cost_estimate=pl.CostEstimate(
             flops=400_000_000, bytes_accessed=1_500_000, transcendentals=200_000

time: 28.4 us -> 23.6 us (0.83)
  local copies, waits for them, and re-layouts: 6.75 us -> 2.23 us
    unnamed x20 -> x4, local copies, waits for them, and re-layouts: 6.75 us -> 2.23 us
where the time goes in v2:
time: 23.6 us; the launch traced here: 23.5 us
  Pallas kernels  20.6 us (87%)
  local copies, waits for them, and re-layouts  2.23 us (9%)
  between operations  0.65 us (3%)
    pallas_call x1, Pallas kernels, shards(): pl.pallas_call(functools.partial(kernel, Z, R), out_shape=(jax.ShapeDtype...  20.6 us
    unnamed x4, local copies, waits for them, and re-layouts  2.23 us

profile of v2, /device:TPU:0, one launch (start us, length us, event | category | flops | bytes accessed | tf_op | source)
XLA Modules:
  0.0 23.5 jit_solution(8744581551446646950)
XLA Ops:
  0.6 20.6 %shard_map.113 = (bf16[16,16,256]{2,1,0:T(8,128)(2,1)}, bf16[16,16,128]{2,1,0:T(8,128)(2,1)}) custom-call(bf16[16,16,256]{2,1,0:T(8,128)(2,1)} %x_hbm.1, bf16[16,16,128]{2,1,0:T(8,128)(2,1)} %edge_hbm.1, s32[16,16]{1,0:T(8,128)} %homolog_hbm.1, s32[16]{0:T(128)} %amino_hbm.1, f32[256]{0:T(256)} %stretch_hbm.1, bf16[256,1024]{1,0:T(8,128)(2,1)} %qkvg_hbm.1, ...), custom_call_target="tpu_custom_call" | custom-call | flops 400000000 | bytes 1500000 | tf_op jit(solution)/shard_map/pallas_call | solution.py:394
  21.2 0.0 copy-start
  21.2 1.6 %copy.14 = bf16[16,16,256]{2,1,0:T(8,128)(2,1)} copy(bf16[16,16,256]{2,1,0:T(8,128)(2,1)} %get-tuple-element.4) | data formatting | bytes 262144
  22.8 0.0 copy-done
  22.8 0.6 %copy.15 = bf16[16,16,128]{2,1,0:T(8,128)(2,1)} copy(bf16[16,16,128]{2,1,0:T(8,128)(2,1)S(1)} %copy-done) | data formatting | bytes 131072
Async XLA Ops:
  21.2 1.6 %copy-start = (bf16[16,16,128]{2,1,0:T(8,128)(2,1)S(1)}, bf16[16,16,128]{2,1,0:T(8,128)(2,1)}, u32[]{:S(2)}) copy-start(bf16[16,16,128]{2,1,0:T(8,128)(2,1)} %get-tuple-element.5) | copy-start | bytes 196612

commit v3 on v2

--- a/solution.py
+++ b/solution.py
@@ -258,6 +258,11 @@
             device_id_type=MESH,
         )
 
+    own_out = pltpu.make_async_copy(ybuf.at[r], y_hbm.at[pl.ds(r * S, S)], local_sem.at[0])
+    own_out.start()
+    for k in range(1, R):
+        y_copy(k).start()
+
     outer_normed = standardize(stack.astype(F32)).astype(BF16)
     factors = dot(outer_normed, operand)
     diagonal = iota((L, L), 0) == iota((L, L), 1)
@@ -310,10 +315,6 @@
         return carry
 
     lax.fori_loop(1, D, send_factors, 0)
-    own_out = pltpu.make_async_copy(ybuf.at[r], y_hbm.at[pl.ds(r * S, S)], local_sem.at[0])
-    own_out.start()
-    for k in range(1, R):
-        y_copy(k).start()
     block_of_columns = z * C // I
     gbuf[me, :, 0:128] = lbuf[r]
     gbuf[me, :, 128:256] = rbuf[block_of_columns]

time: 23.6 us -> 23.6 us (level)
  no operation moved by 1% of the time
where the time goes in v3:
time: 23.6 us; the launch traced here: 23.5 us
  Pallas kernels  20.6 us (87%)
  local copies, waits for them, and re-layouts  2.23 us (9%)
  between operations  0.65 us (3%)
    pallas_call x1, Pallas kernels, shards(): pl.pallas_call(functools.partial(kernel, Z, R), out_shape=(jax.ShapeDtype...  20.6 us
    unnamed x4, local copies, waits for them, and re-layouts  2.23 us

profile of v3, /device:TPU:0, one launch (start us, length us, event | category | flops | bytes accessed | tf_op | source)
XLA Modules:
  0.0 23.5 jit_solution(6850712465356119252)
XLA Ops:
  0.6 20.6 %shard_map.113 = (bf16[16,16,256]{2,1,0:T(8,128)(2,1)}, bf16[16,16,128]{2,1,0:T(8,128)(2,1)}) custom-call(bf16[16,16,256]{2,1,0:T(8,128)(2,1)} %x_hbm.1, bf16[16,16,128]{2,1,0:T(8,128)(2,1)} %edge_hbm.1, s32[16,16]{1,0:T(8,128)} %homolog_hbm.1, s32[16]{0:T(128)} %amino_hbm.1, f32[256]{0:T(256)} %stretch_hbm.1, bf16[256,1024]{1,0:T(8,128)(2,1)} %qkvg_hbm.1, ...), custom_call_target="tpu_custom_call" | custom-call | flops 400000000 | bytes 1500000 | tf_op jit(solution)/shard_map/pallas_call | solution.py:395
  21.2 0.0 copy-start
  21.2 1.6 %copy.14 = bf16[16,16,256]{2,1,0:T(8,128)(2,1)} copy(bf16[16,16,256]{2,1,0:T(8,128)(2,1)} %get-tuple-element.4) | data formatting | bytes 262144
  22.8 0.0 copy-done
  22.8 0.6 %copy.15 = bf16[16,16,128]{2,1,0:T(8,128)(2,1)} copy(bf16[16,16,128]{2,1,0:T(8,128)(2,1)S(1)} %copy-done) | data formatting | bytes 131072
Async XLA Ops:
  21.2 1.6 %copy-start = (bf16[16,16,128]{2,1,0:T(8,128)(2,1)S(1)}, bf16[16,16,128]{2,1,0:T(8,128)(2,1)}, u32[]{:S(2)}) copy-start(bf16[16,16,128]{2,1,0:T(8,128)(2,1)} %get-tuple-element.5) | copy-start | bytes 196612
